TPU v7x, 32 devices: a whole 2x2x4 slice. The times are simulated.
32 devices in a mesh: pairs: 8 (over y, x, core), day: 4 (over z).
Axes of the slice: x: 2, y: 2, z: 4, core: 2. Of those that a mesh axis runs over, the one named last changes fastest.
Arguments:
- spectra: bfloat16 [4, 2, 256, 18432], P('day', None, 'pairs'), may hold values from -6 to 6
- station_row: int32 [256], replicated, may hold values from 0 to 255, as said below
- needed: int32 [128], P('pairs'), may hold values from 0 to 255, as said below
- pair_list: int32 [512, 2], P('pairs'), may hold values from 0 to 15, as said below
- counts: int32 [8], P('pairs'), may hold values from 32 to 64, as said below
Outputs:
- correlations: float32 [512, 1024], P(('pairs', 'day'))
Inputs may be any that keep to these rules, and one draw needn't show every extreme that they name: `station_row`: A permutation of the stations: each row of the spectra belongs to exactly one station. `needed`: each block's 16 entries are distinct stations; at most 4 of one block's stations have their rows on any one index of pairs, and in every block some index of pairs holds exactly 4 of them. `pair_list`: the two positions of a slot differ; empty slots also hold valid positions. `counts`: the live slots of a block are its first ones; in every draw some block has all 64 slots live.
All inputs are finite; a program needn't handle non-finite values.
Results may differ from a plain program's by a relative error of at most 0.013.
Values may be sent and summed in bfloat16 or wider, within the bound.
A program may use at most 128 MiB of HBM per device.

v0:
```python
import math

import jax
import jax.numpy as jnp
from jax import lax
from jax.sharding import PartitionSpec as P

F = 18432
LAGS = 1024
KLO = 720
NFFT = 72000
CAP = 4


TWO_PI = 2.0 * math.pi
FLOOR = 0.25


def angle_rows(first_bin, width):
    bins_here = first_bin + jnp.arange(width, dtype=jnp.int32)
    shifts = jnp.arange(LAGS, dtype=jnp.int32) - LAGS // 2
    phases = jnp.mod(bins_here[:, None] * shifts[None, :], NFFT).astype(jnp.float32) * (
        TWO_PI / NFFT
    )
    return (jnp.cos(phases), jnp.sin(phases))


def to_lags(stack_real, stack_imag, bin_start):
    width_all = stack_real.shape[1]
    block_width = math.gcd(width_all, 512)
    low_cos, low_sin = angle_rows(0, block_width)

    def add_block(index, total):
        offset = index * block_width
        high_cos, high_sin = angle_rows(KLO + bin_start + offset, 1)
        cosine = (high_cos * low_cos - high_sin * low_sin).astype(jnp.bfloat16)
        sine = (high_sin * low_cos + high_cos * low_sin).astype(jnp.bfloat16)
        part_real = lax.dynamic_slice_in_dim(stack_real, offset, block_width, 1)
        part_imag = lax.dynamic_slice_in_dim(stack_imag, offset, block_width, 1)
        total = total + jnp.dot(part_real, cosine, preferred_element_type=jnp.float32)
        return total - jnp.dot(part_imag, sine, preferred_element_type=jnp.float32)

    empty = jnp.zeros((stack_real.shape[0], LAGS), jnp.float32)
    total = lax.fori_loop(0, width_all // block_width, add_block, empty)
    return total * (8.0 / math.sqrt(F))


def owner_ranks(owners):
    length = owners.shape[-1]
    earlier = jnp.arange(length)[None, :] < jnp.arange(length)[:, None]
    same = owners[..., :, None] == owners[..., None, :]
    return jnp.sum(jnp.logical_and(same, earlier), axis=-1)


def make_stack(sums, first_slot, live_count, days):
    slots_here = first_slot + jnp.arange(sums.shape[0], dtype=jnp.int32)
    live = (slots_here < live_count).astype(jnp.float32)[:, None]
    coherence = (sums[:, 2] * sums[:, 2] + sums[:, 3] * sums[:, 3]) / (days * days)
    factor = coherence * live
    stack_real = (sums[:, 0] / days * factor).astype(jnp.bfloat16)
    stack_imag = (sums[:, 1] / days * factor).astype(jnp.bfloat16)
    return (stack_real, stack_imag)


def day_terms(left, right):
    cross_real = left[0] * right[0] + left[1] * right[1]
    cross_imag = left[1] * right[0] - left[0] * right[1]
    divisor = jnp.maximum(jnp.sqrt(cross_real * cross_real + cross_imag * cross_imag), FLOOR)
    return jnp.stack([cross_real, cross_imag, cross_real / divisor, cross_imag / divisor], axis=1)


def shards(spectra, station_row, needed, pair_list, counts):
    holders = lax.axis_size("pairs")
    days_here = lax.axis_size("day")
    stations_here = spectra.shape[2]
    slot_count = pair_list.shape[0]
    my_rows = station_row[needed]
    my_owner = my_rows // stations_here
    my_rank = owner_ranks(my_owner)
    my_slot = my_owner * CAP + my_rank
    onehot = my_slot[:, None] == jnp.arange(holders * CAP, dtype=jnp.int32)[None, :]
    asked = jnp.sum(jnp.where(onehot, (my_rows % stations_here)[:, None], 0), axis=0)
    wanted = lax.all_to_all(
        asked.reshape(holders, CAP), "pairs", split_axis=0, concat_axis=0, tiled=True
    )
    day_count = spectra.shape[0]
    bins_all = spectra.shape[3]
    outgoing = jnp.take(spectra, wanted.reshape(-1), axis=2).reshape(
        day_count, 2, holders, CAP, bins_all
    )
    incoming = lax.all_to_all(outgoing, "pairs", split_axis=2, concat_axis=2, tiled=True)
    mine_spec = jnp.take(incoming.reshape(day_count, 2, holders * CAP, bins_all), my_slot, axis=2)
    first = jnp.take(mine_spec, pair_list[:, 0], axis=2)
    second = jnp.take(mine_spec, pair_list[:, 1], axis=2)
    share = slot_count // days_here
    live_count = counts[0]
    left = first[0].astype(jnp.float32)
    right = second[0].astype(jnp.float32)
    sums = lax.psum_scatter(
        day_terms(left, right).astype(jnp.bfloat16), "day", scatter_dimension=0, tiled=True
    ).astype(jnp.float32)
    first_slot = lax.axis_index("day") * share
    stack_real, stack_imag = make_stack(sums, first_slot, live_count, days_here)
    return to_lags(stack_real, stack_imag, 0)


def solution(mesh):
    in_specs = (P("day", None, "pairs", None), P(), P("pairs"), P("pairs", None), P("pairs"))
    out_specs = P(("pairs", "day"), None)
    return jax.shard_map(shards, mesh=mesh, in_specs=in_specs, out_specs=out_specs, check_vma=False)
```

profile of v0, /device:TPU:0, one launch (start us, length us, event | category | flops | bytes accessed | tf_op | source)
XLA Modules:
  0.0 1182.2 jit_solution(6503301249137884689)
XLA Ops:
  37.4 28.6 %all-to-all-done.1 = bf16[1,2,8,4,18432]{4,1,3,0,2:T(2,128)(2,1)S(1)} async-done(((bf16[1,2,8,4,18432]{4,1,3,0,2:T(2,128)(2,1)}), bf16[1,2,8,4,18432]{4,1,3,0,2:T(2,128)(2,1)S(1)}, u32[]{:S(2)}, u32[]{:S(2)}) %all-to-all-start.1) | async-done | bytes 2359328 | tf_op jit(solution)/shard_map/all_to_all | solution.py:91
  70.0 11.8 gather_fusion.3
  81.8 11.8 gather_fusion.4
  93.6 16.3 %fusion.40 = (f32[1,2,64,18432]{3,2,1,0:T(8,128)}, f32[1,2,64,18432]{3,2,1,0:T(8,128)}) fusion(bf16[64,2,18432]{2,1,0:T(2,128)(2,1)} %gather_fusion.4, pred[64]{0:T(512)(128)(4,1)S(1)} %copy-done.3, bf16[64,2,18432]{2,1,0:T(2,128)(2,1)} %gather_fusion.3, pred[64]{0:T(512)(128)(4,1)S(1)} %copy-done.2), kind=kLoop, calls=%fused_computation.49 | loop fusion | flops 9437184 | bytes 28311680 | tf_op jit(solution)/shard_map/convert_element_type | solution.py:98
  130.4 322.2 %all-reduce.3.cloned.1.call-done = bf16[64,4,18432]{2,1,0:T(4,128)(2,1)} async-done(((bf16[64,4,18432]{2,1,0:T(4,128)(2,1)}), bf16[64,4,18432]{2,1,0:T(4,128)(2,1)}) %all-reduce.3.cloned.1.call-update) | async-done | bytes 9437200
  459.8 714.9 %while.19 = (s32[]{:T(128)}, f32[16,1024]{1,0:T(8,128)S(1)}, bf16[16,18432]{1,0:T(8,128)(2,1)S(1)}, bf16[16,18432]{1,0:T(8,128)(2,1)S(1)}, s32[1024]{0:T(1024)S(...) while((s32[]{:T(128)}, f32[16,1024]{1,0:T(8,128)S(1)}, ...), condition=%wide.region_4.6_spmd.clone.clone.clone.clone, body=%wide.region_3.5_spmd.clone.clone.clone.clone.sunk | while | flops 47245320 | bytes 327861 | solution.py:44
  459.8 9.9 convolution_add_fusion.2
  469.8 9.9 convolution_subtract_fusion.2
  479.7 9.9 convolution_add_fusion.2
  489.6 9.9 convolution_subtract_fusion.2
  499.6 9.9 convolution_add_fusion.2
  509.5 9.9 convolution_subtract_fusion.2
  519.4 9.9 convolution_add_fusion.2
  529.3 9.9 convolution_subtract_fusion.2
  539.3 9.9 convolution_add_fusion.2
  549.2 9.9 convolution_subtract_fusion.2
  559.1 9.9 convolution_add_fusion.2
  579.0 9.9 convolution_add_fusion.2
  588.9 9.9 convolution_subtract_fusion.2
  598.9 9.9 convolution_add_fusion.2
  608.8 9.9 convolution_subtract_fusion.2
  618.7 9.9 convolution_add_fusion.2
  628.6 9.9 convolution_subtract_fusion.2
  638.6 9.9 convolution_add_fusion.2
  658.4 9.9 convolution_add_fusion.2
  668.3 9.9 convolution_subtract_fusion.2
  678.3 9.9 convolution_add_fusion.2
  688.2 9.9 convolution_subtract_fusion.2
  698.1 9.9 convolution_add_fusion.2
  708.0 9.9 convolution_subtract_fusion.2
  718.0 9.9 convolution_add_fusion.2
  727.9 9.9 convolution_subtract_fusion.2
  737.9 9.9 convolution_add_fusion.2
  747.8 9.9 convolution_subtract_fusion.2
  757.7 9.9 convolution_add_fusion.2
  767.6 9.9 convolution_subtract_fusion.2
  777.6 9.9 convolution_add_fusion.2
  787.5 9.9 convolution_subtract_fusion.2
  797.4 9.9 convolution_add_fusion.2
  807.3 9.9 convolution_subtract_fusion.2
  817.3 9.9 convolution_add_fusion.2
  827.2 9.9 convolution_subtract_fusion.2
  837.1 9.9 convolution_add_fusion.2
  847.1 9.9 convolution_subtract_fusion.2
  857.0 9.9 convolution_add_fusion.2
  866.9 9.9 convolution_subtract_fusion.2
  876.9 9.9 convolution_add_fusion.2
  886.8 9.9 convolution_subtract_fusion.2
  896.7 9.9 convolution_add_fusion.2
  906.6 9.9 convolution_subtract_fusion.2
  916.6 9.9 convolution_add_fusion.2
  926.5 9.9 convolution_subtract_fusion.2
  936.4 9.9 convolution_add_fusion.2
  956.3 9.9 convolution_add_fusion.2
  976.2 9.9 convolution_add_fusion.2
  996.0 9.9 convolution_add_fusion.2
  1015.9 9.9 convolution_add_fusion.2
  1035.7 9.9 convolution_add_fusion.2
  1055.6 9.9 convolution_add_fusion.2
  1075.4 9.9 convolution_add_fusion.2
  1095.3 9.9 convolution_add_fusion.2
  1115.2 9.9 convolution_add_fusion.2
  1135.0 9.9 convolution_add_fusion.2
  1154.9 9.9 convolution_add_fusion.2
  (105 shorter events, 202.2 us)
Async XLA Ops:
  6.5 0.7 copy-start
  8.9 10.7 all-to-all-start
  32.2 4.6 copy-start.4
  32.2 33.8 %all-to-all-start.1 = ((bf16[1,2,8,4,18432]{4,1,3,0,2:T(2,128)(2,1)}), bf16[1,2,8,4,18432]{4,1,3,0,2:T(2,128)(2,1)S(1)}, u32[]{:S(2)}, u32[]{:S(2)}) async-start(bf16[1,2,8,4,18432]{4,1,3,0,2:T(2,128)(2,1)} %broadcast_select_fusion), calls=%async_computation.1 | async-start | bytes 4718592 | tf_op jit(solution)/shard_map/all_to_all | solution.py:91
  36.5 416.1 %all-reduce.3.cloned.1.call-start = ((), (), s32[]{:S(2)}) async-start(), calls=%async_computation.2 | async-start | bytes 18874368
  81.8 11.8 copy-start.2
  81.8 11.8 copy-start.3
  128.4 0.7 copy-start.5
  1174.7 0.7 copy-start.1
Sparse Core Ops, SparseCore 0:
  128.5 324.0 all-reduce.2
where the time goes:
time: 1180 us
  matrix products  712 us (60%)
  waiting for transfers between devices  351 us (30%)
  local copies, waits for them, and re-layouts  49.8 us (4%)
  other arithmetic  44.2 us (4%)
  between operations  14.9 us (1%)
    dot_general x36, matrix products, add_block(): jnp.dot(part_real, cosine, preferred_element_type=jnp.float32)  357 us
    dot_general x36, matrix products, add_block(): return total - jnp.dot(part_imag, sine, preferred_element_type=jnp.float32)  356 us
    unnamed x2, waiting for transfers between devices  322 us
    all_to_all x1, waiting for transfers between devices, shards(): lax.all_to_all(outgoing, 'pairs', split_axis=2, concat_axis=2, tiled=True)  28.6 us
  transfers between devices with their start and end apart: 3, of which 2 were waited for; matrix products, arithmetic and copies ran while one was open for 1% of the time, Pallas kernels for 0%

commit v1 on v0

v1 whole, which is shorter than its diff:
```python
import functools
import math

import jax
import jax.numpy as jnp
import numpy as np
from jax import lax
from jax.experimental import pallas as pl
from jax.experimental.pallas import tpu as pltpu
from jax.sharding import PartitionSpec as P

LAGS = 1024
KLO = 720
NFFT = 72000
CAP = 4
HALF = LAGS // 2
FLOOR = 0.25
MESH = pl.DeviceIdType.MESH


def lag_constants(bins, days, block):
    odd = 2 * np.arange(HALF, dtype=np.int64) + 1

    def angle(steps):
        return (np.mod(steps, 2 * NFFT) * (math.pi / NFFT)).astype(np.float64)

    inner = angle(np.arange(block, dtype=np.int64)[:, None] * odd[None, :])
    table = np.concatenate([np.cos(inner), np.sin(inner)], axis=1).astype(jnp.bfloat16)
    starts = KLO + np.arange(0, bins, block, dtype=np.int64)
    outer = angle(starts[:, None] * odd[None, :])
    outer = np.stack([np.cos(outer), np.sin(outer)], axis=1).astype(np.float32)
    turn = angle(KLO + np.arange(bins, dtype=np.int64))
    turn = np.stack([np.cos(turn), np.sin(turn)]).astype(np.float32)
    turn = turn.reshape(2, days, bins // days).transpose(1, 0, 2)
    return table, outer.reshape(days, -1, 2, HALF), turn


def kernel(
    holders, days, spec, req, comp, sel, table, outer, turn, out,
    reqin, outbox, inbox, zout, zin, stack, even, odd, part, shares,
    qsend, qrecv, xsend, xrecv, zsend, zrecv, rsend, rrecv,
):
    me, day = lax.axis_index("pairs"), lax.axis_index("day")
    width = outbox.shape[2]
    need4 = zin.shape[1]
    slots = part.shape[0]
    share = slots // days
    block = table.shape[0]
    tile = 256 if block % 256 == 0 else 128
    blocks = 2 * width // block

    def xy(p):
        return lax.rem(me + p, holders)

    def zz(s):
        return lax.rem(day + s, days)

    def rows16(b):
        return pl.ds(pl.multiple_of(b * 16, 16), 16)

    def remote(src, dst, ssem, rsem, dev):
        return pltpu.make_async_remote_copy(
            src_ref=src, dst_ref=dst, send_sem=ssem, recv_sem=rsem, device_id=dev, device_id_type=MESH
        )

    def ask(p):
        return remote(req.at[rows16(xy(p))], reqin.at[rows16(me)], qsend.at[p], qrecv.at[p], (xy(p), day))

    def give(f, p):
        return remote(
            outbox.at[f, rows16(xy(p))], inbox.at[f, rows16(me)], xsend.at[f, p], xrecv.at[f, p], (xy(p), day)
        )

    def pass_on(s):
        return remote(zout.at[zz(s)], zin.at[day], zsend.at[s], zrecv.at[s], (me, zz(s)))

    def hand(s):
        rows = pl.ds(pl.multiple_of(zz(s) * share, share), share)
        return remote(part.at[rows], shares.at[day], rsend.at[s], rrecv.at[s], (me, zz(s)))

    barrier = pltpu.get_barrier_semaphore()
    for p in range(1, holders):
        pl.semaphore_signal(barrier, inc=1, device_id=(xy(p), day), device_id_type=MESH)
    for s in range(1, days):
        pl.semaphore_signal(barrier, inc=1, device_id=(me, zz(s)), device_id_type=MESH)
    pl.semaphore_wait(barrier, holders + days - 2)

    for p in range(1, holders):
        ask(p).start()
    reqin[rows16(me)] = req[rows16(me)]
    for p in range(1, holders):
        ask(p).wait()
    lanes = lax.broadcasted_iota(jnp.int32, reqin.shape, 1)
    pick = jnp.where(reqin[...] == lanes, 1.0, 0.0).astype(jnp.bfloat16)

    def send_step(step, carry):
        f = lax.rem(day + 1 + step, days)
        parts = []
        for h in range(2):
            cols = pl.ds(pl.multiple_of((2 * f + h) * width, 128), width)
            for c in range(2):
                parts.append(spec[c, :, cols])
        picked = jnp.dot(pick, jnp.concatenate(parts, axis=0), preferred_element_type=jnp.float32)
        outbox[f] = picked.astype(jnp.bfloat16)
        for p in range(1, holders):
            give(f, p).start()
        inbox[f, rows16(me)] = outbox[f, rows16(me)]
        return carry

    lax.fori_loop(0, days, send_step, 0)

    for s in range(1, days + 1):
        f = zz(s)
        for p in range(1, holders):
            give(f, p).wait_recv()
        packed = jnp.dot(comp[...], inbox[f], preferred_element_type=jnp.float32).astype(jnp.bfloat16)
        if s < days:
            zout[f] = packed
            pass_on(s).start()
        else:
            zin[day] = packed

    even[...] = jnp.zeros_like(even)
    odd[...] = jnp.zeros_like(odd)
    for s in range(1, days):
        pass_on(s).wait_recv()

    def block_step(n, carry):
        half = n // (blocks // 2)
        base = (n - half * (blocks // 2)) * block
        rows = pl.ds(pl.multiple_of(half * (need4 // 2), 16), need4 // 2)

        def tile_step(t, inner):
            cols = pl.ds(pl.multiple_of(base + t * tile, 128), tile)
            sums = None
            for d in range(days):
                both = jnp.dot(sel[...], zin[d, rows, cols], preferred_element_type=jnp.float32)
                a, b = both[:slots], both[slots : 2 * slots]
                c, e = both[2 * slots : 3 * slots], both[3 * slots :]
                real = a * c + b * e
                imag = b * c - a * e
                inv = lax.rsqrt(jnp.maximum(real * real + imag * imag, FLOOR * FLOOR))
                terms = (real, imag, real * inv, imag * inv)
                sums = terms if sums is None else tuple(x + y for x, y in zip(sums, terms))
            coherence = sums[2] * sums[2] + sums[3] * sums[3]
            real, imag = sums[0] * coherence, sums[1] * coherence
            at = pl.ds(pl.multiple_of(n * block + t * tile, 128), tile)
            cos, sin = turn[day, 0:1, at], turn[day, 1:2, at]
            to = pl.ds(pl.multiple_of(t * tile, 128), tile)
            stack[0:slots, to] = (real * cos + imag * sin).astype(jnp.bfloat16)
            stack[slots : 2 * slots, to] = (imag * cos - real * sin).astype(jnp.bfloat16)
            return inner

        lax.fori_loop(0, block // tile, tile_step, 0)
        z = jnp.dot(stack[...], table[...], preferred_element_type=jnp.float32)
        cos, sin = outer[day, n, 0:1, :], outer[day, n, 1:2, :]
        even[...] += cos * z[:slots, :HALF] - sin * z[:slots, HALF:]
        odd[...] += sin * z[slots:, :HALF] + cos * z[slots:, HALF:]
        return carry

    lax.fori_loop(0, blocks, block_step, 0)

    flip = lax.broadcasted_iota(jnp.int32, (HALF, HALF), 0) + lax.broadcasted_iota(jnp.int32, (HALF, HALF), 1)
    flip = jnp.where(flip == HALF - 1, 1.0, 0.0)
    part[:, HALF:] = even[...] - odd[...]
    part[:, :HALF] = jnp.dot(
        even[...] + odd[...], flip, precision=lax.Precision.HIGHEST, preferred_element_type=jnp.float32
    )
    for s in range(1, days):
        hand(s).start()
    shares[day] = part[pl.ds(pl.multiple_of(day * share, share), share)]
    for s in range(1, days):
        hand(s).wait_recv()
    total = shares[0]
    for d in range(1, days):
        total = total + shares[d]
    out[...] = total

    for s in range(1, days):
        hand(s).wait_send()
        pass_on(s).wait_send()
    for s in range(1, days + 1):
        for p in range(1, holders):
            give(zz(s), p).wait_send()


def shards(days, holders, spectra, station_row, needed, pair_list, counts):
    stations = spectra.shape[2]
    bins = spectra.shape[3]
    need = needed.shape[0]
    slots = pair_list.shape[0]
    width = bins // days // 2
    block = width // 3
    names = jnp.arange(station_row.shape[0], dtype=jnp.int32)
    my_rows = jnp.sum(jnp.where(needed[:, None] == names[None, :], station_row[None, :], 0), axis=1)
    owner = my_rows // stations
    local = my_rows % stations
    places = jnp.arange(need, dtype=jnp.int32)
    earlier = places[None, :] < places[:, None]
    rank = jnp.sum(jnp.logical_and(owner[:, None] == owner[None, :], earlier), axis=1).astype(jnp.int32)
    my_slot = owner * CAP + rank

    where_is = jnp.arange(holders * CAP, dtype=jnp.int32)
    asked = jnp.sum(jnp.where(where_is[:, None] == my_slot[None, :], local[None, :] + 1, 0), axis=1) - 1
    asked = asked.reshape(holders, 1, CAP)
    quarter = jnp.arange(4, dtype=jnp.int32)
    req = jnp.where(asked >= 0, quarter[None, :, None] * stations + asked, -1)
    req = jnp.broadcast_to(req.reshape(holders * 16, 1), (holders * 16, 4 * stations))

    comp = (owner * 16 + rank)[None, :] + (quarter * CAP)[:, None]
    comp = comp.reshape(4 * need, 1) == jnp.arange(holders * 16, dtype=jnp.int32)[None, :]
    comp = comp.astype(jnp.bfloat16)
    kinds = pair_list.T[:, None, :] + (jnp.arange(2, dtype=jnp.int32) * need)[None, :, None]
    sel = kinds.reshape(4 * slots, 1) == jnp.arange(2 * need, dtype=jnp.int32)[None, :]
    sel = sel.astype(jnp.bfloat16)

    table, outer, turn = lag_constants(bins, days, block)
    bf, f32 = jnp.bfloat16, jnp.float32
    dma = pltpu.SemaphoreType.DMA
    vmem = pl.BlockSpec(memory_space=pltpu.VMEM)
    summed = pl.pallas_call(
        functools.partial(kernel, holders, days),
        out_shape=jax.ShapeDtypeStruct((slots // days, LAGS), f32),
        in_specs=[vmem] * 7,
        out_specs=vmem,
        scratch_shapes=[
            pltpu.VMEM((holders * 16, 4 * stations), jnp.int32),
            pltpu.VMEM((days, holders * 16, width), bf),
            pltpu.VMEM((days, holders * 16, width), bf),
            pltpu.VMEM((days, 4 * need, width), bf),
            pltpu.VMEM((days, 4 * need, width), bf),
            pltpu.VMEM((2 * slots, block), bf),
            pltpu.VMEM((slots, HALF), f32),
            pltpu.VMEM((slots, HALF), f32),
            pltpu.VMEM((slots, LAGS), f32),
            pltpu.VMEM((days, slots // days, LAGS), f32),
            dma((holders,)), dma((holders,)),
            dma((days, holders)), dma((days, holders)),
            dma((days,)), dma((days,)),
            dma((days,)), dma((days,)),
        ],
        compiler_params=pltpu.CompilerParams(
            collective_id=0, has_side_effects=True, vmem_limit_bytes=48 * 2**20
        ),
    )(spectra[0], req, comp, sel, jnp.asarray(table), jnp.asarray(outer), jnp.asarray(turn))
    share = slots // days
    mine = lax.axis_index("day") * share + jnp.arange(share, dtype=jnp.int32)
    scale = 8.0 / math.sqrt(bins) / float(days) ** 3
    return jnp.where((mine < counts[0])[:, None], summed * scale, 0.0)


def solution(mesh):
    in_specs = (P("day", None, "pairs", None), P(), P("pairs"), P("pairs", None), P("pairs"))
    out_specs = P(("pairs", "day"), None)
    body = functools.partial(shards, mesh.shape["day"], mesh.shape["pairs"])
    return jax.shard_map(body, mesh=mesh, in_specs=in_specs, out_specs=out_specs, check_vma=False)
```

time: 1180 us -> 68.8 us (0.06)
  matrix products: 712 us -> 0 us
  waiting for transfers between devices: 351 us -> 0 us
  Pallas kernels: 0 us -> 59.4 us
  local copies, waits for them, and re-layouts: 49.8 us -> 5.31 us
  other arithmetic: 44.2 us -> 2.98 us
  between operations: 14.9 us -> 0.72 us
    dot_general x72 -> x0, matrix products: 712 us -> none  [the longest x36 357 us: add_block(): jnp.dot(part_real, cosine, preferred_element_type=jnp.float32)]
    unnamed x2 -> x0, waiting for transfers between devices: 322 us -> none
    pallas_call x0 -> x1, Pallas kernels: none -> 59.4 us  [shards(): pl.pallas_call(functools.partial(kernel, holders, days), out_shape=jax.Sh...]
    gather x5 -> x0, local copies, waits for them, and re-layouts: 34.8 us -> none  [the longest x1 11.8 us: shards(): second = jnp.take(mine_spec, pair_list[:, 1], axis=2)]
    all_to_all x2 -> x0, waiting for transfers between devices: 28.6 us -> none  [the longest x1 28.6 us: shards(): lax.all_to_all(outgoing, 'pairs', split_axis=2, concat_axis=2, tiled=True)]
    convert_element_type x3 -> x2, other arithmetic: 19.8 us -> 0.18 us  [the longest x1 0.1 us: shards(): sel = sel.astype(jnp.bfloat16)]
    another operation x4 -> x0, other arithmetic: 12.2 us -> none
  transfers between devices with their start and end apart: 3 -> 0, of which waited for: 2 -> 0; matrix products, arithmetic and copies ran while one was open for 1% -> 0% of each run, Pallas kernels for 0% -> 0%
where the time goes in v1:
time: 68.8 us; the launch traced here: 68.4 us
  Pallas kernels  59.4 us (86%)
  local copies, waits for them, and re-layouts  5.31 us (8%)
  other arithmetic  2.98 us (4%)
  between operations  0.72 us (1%)
    pallas_call x1, Pallas kernels, shards(): pl.pallas_call(functools.partial(kernel, holders, days), out_shape=jax.Sh...  59.4 us
    unnamed x8, local copies, waits for them, and re-layouts  4.87 us

profile of v1, /device:TPU:0, one launch (start us, length us, event | category | flops | bytes accessed | tf_op | source)
XLA Modules:
  0.0 68.4 jit_solution(2348262574831067698)
XLA Ops:
  0.0 0.9 %select_reduce_fusion = s32[16]{0:T(128)S(1)} fusion(s32[256]{0:T(256)} %param.9, s32[16]{0:T(128)} %param.10), kind=kLoop, calls=%fused_computation.6 | loop fusion | flops 12272 | bytes 1152 | tf_op jit(solution)/shard_map/reduce_sum | solution.py:195
  0.9 0.2 convert_reduce_fusion
  1.1 0.1 select_reduce_fusion.1
  1.2 0.1 sub.12
  1.3 0.1 add_select_fusion
  1.3 0.1 select_n.58
  1.5 0.1 broadcast_in_dim.78.req
  1.6 0.1 broadcast_add_fusion.1
  1.6 0.1 add.137
  1.7 0.1 fusion.1.comp
  1.8 0.8 %broadcast_add_fusion = s32[2,2,64]{2,1,0:T(2,128)S(1)} fusion(s32[2,64]{1,0:T(2,128)} %bitcast.5, s32[2]{0:T(128)S(1)} %iota_multiply_fusion), kind=kLoop, calls=%fused_computation.19 | loop fusion | flops 256 | bytes 1544 | tf_op jit(solution)/shard_map/add | solution.py:213
  2.6 0.1 add.141
  2.6 0.1 fusion.sel
  2.7 0.0 copy-start
  2.8 1.7 %copy-done = bf16[1,2,32,18432]{3,2,1,0:T(8,128)(2,1)S(1)} copy-done((bf16[1,2,32,18432]{3,2,1,0:T(8,128)(2,1)S(1)}, bf16[1,2,32,18432]{3,2,1,0:T(8,128)(2,1)}, u32[]{:S(2)}) %copy-start) | copy-done | bytes 2359320
  4.4 0.0 copy-start.1
  4.4 1.4 %copy-done.1 = bf16[768,1024]{1,0:T(8,128)(2,1)S(1)} copy-done((bf16[768,1024]{1,0:T(8,128)(2,1)S(1)}, bf16[768,1024]{1,0:T(8,128)(2,1)}, u32[]{:S(2)}) %copy-start.1) | copy-done | bytes 1572888
  5.8 0.0 copy-start.2
  5.8 0.9 %copy-done.2 = f32[4,2,4608]{2,1,0:T(2,128)S(1)} copy-done((f32[4,2,4608]{2,1,0:T(2,128)S(1)}, f32[4,2,4608]{2,1,0:T(2,128)}, u32[]{:S(2)}) %copy-start.2) | copy-done | bytes 147480
  6.7 0.0 copy-start.3
  6.7 0.9 %copy-done.3 = f32[4,6,2,512]{3,2,1,0:T(2,128)S(1)} copy-done((f32[4,6,2,512]{3,2,1,0:T(2,128)S(1)}, f32[4,6,2,512]{3,2,1,0:T(2,128)}, u32[]{:S(2)}) %copy-start.3) | copy-done | bytes 98328
  7.6 59.4 %shard_map.82 = f32[16,1024]{1,0:T(8,128)S(1)} custom-call(bf16[2,32,18432]{2,1,0:T(8,128)(2,1)S(1)} %bitcast.4, s32[128,128]{1,0:T(8,128)S(1)} %broadcast_in_dim.78.req, bf16[64,128]{1,0:T(8,128)(2,1)S(1)} %fusion.1.comp, bf16[256,32]{1,0:T(8,128)(2,1)S(1)} %fusion.sel, bf16[768,1024]{1,0:T(8,128)(2,1)S(1)} %copy-done.1, f32[4,6,2,512]{3,2,1,0:T(2,128)S(1)} %copy-done.3, ...), custom_call_target="tpu_custom_call" | custom-call | tf_op jit(solution)/shard_map/pallas_call | solution.py:221
  67.7 0.7 %multiply_select_fusion = f32[16,1024]{1,0:T(8,128)} fusion(f32[16,1024]{1,0:T(8,128)S(1)} %shard_map.82, pred[16]{0:T(512)(128)(4,1)S(1)} %add_compare_fusion), kind=kLoop, calls=%fused_computation.2 | loop fusion | flops 32768 | bytes 131088 | tf_op jit(solution)/shard_map/jit(_where)/select_n | solution.py:249
  (8 shorter events, 0.1 us)
Async XLA Ops:
  2.7 1.7 %copy-start = (bf16[1,2,32,18432]{3,2,1,0:T(8,128)(2,1)S(1)}, bf16[1,2,32,18432]{3,2,1,0:T(8,128)(2,1)}, u32[]{:S(2)}) copy-start(bf16[1,2,32,18432]{3,2,1,0:T(8,128)(2,1)} %param.8) | copy-start | bytes 7077892
  4.4 1.4 %copy-start.1 = (bf16[768,1024]{1,0:T(8,128)(2,1)S(1)}, bf16[768,1024]{1,0:T(8,128)(2,1)}, u32[]{:S(2)}) copy-start(bf16[768,1024]{1,0:T(8,128)(2,1)} %constant.56.clone.table) | copy-start | bytes 4718596
  5.8 0.9 %copy-start.2 = (f32[4,2,4608]{2,1,0:T(2,128)S(1)}, f32[4,2,4608]{2,1,0:T(2,128)}, u32[]{:S(2)}) copy-start(f32[4,2,4608]{2,1,0:T(2,128)} %constant.58.clone.turn) | copy-start | bytes 442372
  6.7 0.9 %copy-start.3 = (f32[4,6,2,512]{3,2,1,0:T(2,128)S(1)}, f32[4,6,2,512]{3,2,1,0:T(2,128)}, u32[]{:S(2)}) copy-start(f32[4,6,2,512]{3,2,1,0:T(2,128)} %constant.57.clone.outer) | copy-start | bytes 294916

commit v2 on v1

v2 whole, which is shorter than its diff:
```python
import functools
import math

import jax
import jax.numpy as jnp
import numpy as np
from jax import lax
from jax.experimental import pallas as pl
from jax.experimental.pallas import tpu as pltpu
from jax.sharding import PartitionSpec as P

LAGS = 1024
KLO = 720
NFFT = 72000
CAP = 4
HALF = LAGS // 2
FLOOR = 0.25
CUTS = 3
AHEAD = 4
MESH = pl.DeviceIdType.MESH


def lag_constants(bins, days, block):
    odd = 2 * np.arange(HALF, dtype=np.int64) + 1

    def angle(steps):
        return (np.mod(steps, 2 * NFFT) * (math.pi / NFFT)).astype(np.float64)

    inner = angle(np.arange(block, dtype=np.int64)[:, None] * odd[None, :])
    table = np.concatenate([np.cos(inner), np.sin(inner)], axis=1).astype(jnp.bfloat16)
    starts = KLO + np.arange(0, bins, block, dtype=np.int64)
    outer = angle(starts[:, None] * odd[None, :])
    outer = np.stack([np.cos(outer), np.sin(outer)], axis=1).astype(np.float32)
    turn = angle(KLO + np.arange(bins, dtype=np.int64))
    turn = np.stack([np.cos(turn), np.sin(turn)]).astype(np.float32)
    turn = turn.reshape(2, days, bins // days).transpose(1, 0, 2)
    return table, outer.reshape(days, -1, 2, HALF), turn


def kernel(
    holders, days, cuts, spec_hbm, req, comp, sel, table_hbm, outer_hbm, turn_hbm, out,
    spec, table, outer, turn, reqin, outbox, inbox, zout, zin, stack, even, odd, flip, part, shares,
    lsem, qsend, qrecv, xsend, xrecv, zsend, zrecv, rsend, rrecv,
):
    me, day = lax.axis_index("pairs"), lax.axis_index("day")
    width = outbox.shape[2]
    need4 = zin.shape[2]
    slots = even.shape[0]
    share = slots // days
    units = cuts * days
    tile = 256 if width % 256 == 0 else 128

    def xy(p):
        return lax.rem(me + p, holders)

    def zz(s):
        return lax.rem(day + s, days)

    def rows16(b):
        return pl.ds(pl.multiple_of(b * 16, 16), 16)

    def remote(src, dst, ssem, rsem, dev):
        return pltpu.make_async_remote_copy(
            src_ref=src, dst_ref=dst, send_sem=ssem, recv_sem=rsem, device_id=dev, device_id_type=MESH
        )

    def ask(p):
        return remote(req.at[rows16(xy(p))], reqin.at[rows16(me)], qsend.at[p], qrecv.at[p], (xy(p), day))

    def give(i, p):
        return remote(
            outbox.at[i, rows16(xy(p))], inbox.at[i, rows16(me)], xsend.at[i, p], xrecv.at[i, p], (xy(p), day)
        )

    def pass_on(u, s):
        return remote(zout.at[u, s], zin.at[u, day], zsend.at[u, s], zrecv.at[u, s], (me, zz(s)))

    def hand(s):
        return remote(part.at[zz(s)], shares.at[day], rsend.at[s], rrecv.at[s], (me, zz(s)))

    loads = [
        pltpu.make_async_copy(src, dst, lsem.at[i])
        for i, (src, dst) in enumerate(
            ((spec_hbm, spec), (table_hbm, table), (outer_hbm, outer), (turn_hbm, turn))
        )
    ]
    for load in loads:
        load.start()

    barrier = pltpu.get_barrier_semaphore()
    for p in range(1, holders):
        pl.semaphore_signal(barrier, inc=1, device_id=(xy(p), day), device_id_type=MESH)
    for s in range(1, days):
        pl.semaphore_signal(barrier, inc=1, device_id=(me, zz(s)), device_id_type=MESH)
    pl.semaphore_wait(barrier, holders + days - 2)

    for p in range(1, holders):
        ask(p).start()
    reqin[rows16(me)] = req[rows16(me)]
    across = lax.broadcasted_iota(jnp.int32, (HALF, HALF), 0) + lax.broadcasted_iota(jnp.int32, (HALF, HALF), 1)
    flip[...] = jnp.where(across == HALF - 1, 1.0, 0.0).astype(jnp.bfloat16)
    even[...] = jnp.zeros_like(even)
    odd[...] = jnp.zeros_like(odd)
    loads[0].wait()
    for p in range(1, holders):
        ask(p).wait()
    lanes = lax.broadcasted_iota(jnp.int32, reqin.shape, 1)
    pick = jnp.where(reqin[...] == lanes, 1.0, 0.0).astype(jnp.bfloat16)

    def give_unit(i):
        u, s = i // days, i % days + 1
        parts = []
        for h in range(2):
            at = ((2 * zz(s) + h) * cuts + u) * width
            for c in range(2):
                parts.append(spec[c, :, pl.ds(pl.multiple_of(at, 128), width)])
        picked = jnp.dot(pick, jnp.concatenate(parts, axis=0), preferred_element_type=jnp.float32)
        outbox[i] = picked.astype(jnp.bfloat16)
        for p in range(1, holders):
            give(i, p).start()
        inbox[i, rows16(me)] = outbox[i, rows16(me)]

    def relay_unit(i):
        u, s = i // days, i % days + 1
        for p in range(1, holders):
            give(i, p).wait_recv()
        packed = jnp.dot(comp[...], inbox[i], preferred_element_type=jnp.float32).astype(jnp.bfloat16)
        if s < days:
            zout[u, s] = packed
            pass_on(u, s).start()
        else:
            zin[u, day] = packed

    def add_block(u, h):
        n = h * cuts + u
        rows = pl.ds(h * (need4 // 2), need4 // 2)

        def tile_step(t, inner):
            cols = pl.ds(pl.multiple_of(t * tile, 128), tile)
            sums = None
            for d in range(days):
                both = jnp.dot(sel[...], zin[u, d, rows, cols], preferred_element_type=jnp.float32)
                a, b = both[:slots], both[slots : 2 * slots]
                c, e = both[2 * slots : 3 * slots], both[3 * slots :]
                real = a * c + b * e
                imag = b * c - a * e
                inv = lax.rsqrt(jnp.maximum(real * real + imag * imag, FLOOR * FLOOR))
                terms = (real, imag, real * inv, imag * inv)
                sums = terms if sums is None else tuple(x + y for x, y in zip(sums, terms))
            coherence = sums[2] * sums[2] + sums[3] * sums[3]
            real, imag = sums[0] * coherence, sums[1] * coherence
            at = pl.ds(pl.multiple_of(n * width + t * tile, 128), tile)
            cos, sin = turn[day, 0:1, at], turn[day, 1:2, at]
            stack[0:slots, cols] = (real * cos + imag * sin).astype(jnp.bfloat16)
            stack[slots : 2 * slots, cols] = (imag * cos - real * sin).astype(jnp.bfloat16)
            return inner

        lax.fori_loop(0, width // tile, tile_step, 0)
        z = jnp.dot(stack[...], table[...], preferred_element_type=jnp.float32)
        cos, sin = outer[day, n, 0:1, :], outer[day, n, 1:2, :]
        even[...] += cos * z[:slots, :HALF] - sin * z[:slots, HALF:]
        odd[...] += sin * z[slots:, :HALF] + cos * z[slots:, HALF:]

    for i in range(AHEAD):
        give_unit(i)
    for load in loads[1:]:
        load.wait()
    for i in range(units + days):
        u, s = i // days, i % days + 1
        if i + AHEAD < units:
            give_unit(i + AHEAD)
        if i < units:
            relay_unit(i)
        if u and s == days // 2:
            for z in range(1, days):
                pass_on(u - 1, z).wait_recv()
            add_block(u - 1, 0)
        if u and s == days:
            add_block(u - 1, 1)

    for d in range(days):
        rows = slice(d * share, (d + 1) * share)
        part[d] = jnp.concatenate([even[rows], odd[rows]], axis=0).astype(jnp.bfloat16)
    for s in range(1, days):
        hand(s).start()
    shares[day] = part[day]
    for s in range(1, days):
        hand(s).wait_recv()
    total = shares[0].astype(jnp.float32)
    for d in range(1, days):
        total = total + shares[d].astype(jnp.float32)
    out[:, HALF:] = total[:share] - total[share:]
    left = total[:share] + total[share:]
    turned = None
    for _ in range(3):
        high = left.astype(jnp.bfloat16)
        left = left - high.astype(jnp.float32)
        piece = jnp.dot(high, flip[...], preferred_element_type=jnp.float32)
        turned = piece if turned is None else turned + piece
    out[:, :HALF] = turned

    for s in range(1, days):
        hand(s).wait_send()
        for u in range(cuts):
            pass_on(u, s).wait_send()
    for i in range(units):
        for p in range(1, holders):
            give(i, p).wait_send()


def shards(days, holders, spectra, station_row, needed, pair_list, counts):
    stations = spectra.shape[2]
    bins = spectra.shape[3]
    need = needed.shape[0]
    slots = pair_list.shape[0]
    cuts = CUTS
    units = cuts * days
    block = bins // days // 2 // cuts
    names = jnp.arange(station_row.shape[0], dtype=jnp.int32)
    my_rows = jnp.sum(jnp.where(needed[:, None] == names[None, :], station_row[None, :], 0), axis=1)
    owner = my_rows // stations
    local = my_rows % stations
    places = jnp.arange(need, dtype=jnp.int32)
    earlier = places[None, :] < places[:, None]
    rank = jnp.sum(jnp.logical_and(owner[:, None] == owner[None, :], earlier), axis=1).astype(jnp.int32)
    my_slot = owner * CAP + rank

    where_is = jnp.arange(holders * CAP, dtype=jnp.int32)
    asked = jnp.sum(jnp.where(where_is[:, None] == my_slot[None, :], local[None, :] + 1, 0), axis=1) - 1
    asked = asked.reshape(holders, 1, CAP)
    quarter = jnp.arange(4, dtype=jnp.int32)
    req = jnp.where(asked >= 0, quarter[None, :, None] * stations + asked, -1)
    req = jnp.broadcast_to(req.reshape(holders * 16, 1), (holders * 16, 4 * stations))

    comp = (owner * 16 + rank)[None, :] + (quarter * CAP)[:, None]
    comp = comp.reshape(4 * need, 1) == jnp.arange(holders * 16, dtype=jnp.int32)[None, :]
    comp = comp.astype(jnp.bfloat16)
    kinds = pair_list.T[:, None, :] + (jnp.arange(2, dtype=jnp.int32) * need)[None, :, None]
    sel = kinds.reshape(4 * slots, 1) == jnp.arange(2 * need, dtype=jnp.int32)[None, :]
    sel = sel.astype(jnp.bfloat16)

    table, outer, turn = lag_constants(bins, days, block)
    bf, f32 = jnp.bfloat16, jnp.float32
    dma = pltpu.SemaphoreType.DMA
    vmem = pl.BlockSpec(memory_space=pltpu.VMEM)
    hbm = pl.BlockSpec(memory_space=pl.ANY)
    summed = pl.pallas_call(
        functools.partial(kernel, holders, days, cuts),
        out_shape=jax.ShapeDtypeStruct((slots // days, LAGS), f32),
        in_specs=[hbm, vmem, vmem, vmem, hbm, hbm, hbm],
        out_specs=vmem,
        scratch_shapes=[
            pltpu.VMEM(spectra.shape[1:], bf),
            pltpu.VMEM(table.shape, bf),
            pltpu.VMEM(outer.shape, f32),
            pltpu.VMEM(turn.shape, f32),
            pltpu.VMEM((holders * 16, 4 * stations), jnp.int32),
            pltpu.VMEM((units, holders * 16, block), bf),
            pltpu.VMEM((units, holders * 16, block), bf),
            pltpu.VMEM((cuts, days, 4 * need, block), bf),
            pltpu.VMEM((cuts, days, 4 * need, block), bf),
            pltpu.VMEM((2 * slots, block), bf),
            pltpu.VMEM((slots, HALF), f32),
            pltpu.VMEM((slots, HALF), f32),
            pltpu.VMEM((HALF, HALF), bf),
            pltpu.VMEM((days, 2 * slots // days, HALF), bf),
            pltpu.VMEM((days, 2 * slots // days, HALF), bf),
            dma((4,)),
            dma((holders,)), dma((holders,)),
            dma((units, holders)), dma((units, holders)),
            dma((cuts, days)), dma((cuts, days)),
            dma((days,)), dma((days,)),
        ],
        compiler_params=pltpu.CompilerParams(
            collective_id=0, has_side_effects=True, vmem_limit_bytes=48 * 2**20
        ),
    )(spectra[0], req, comp, sel, jnp.asarray(table), jnp.asarray(outer), jnp.asarray(turn))
    share = slots // days
    mine = lax.axis_index("day") * share + jnp.arange(share, dtype=jnp.int32)
    scale = 8.0 / math.sqrt(bins) / float(days) ** 3
    return jnp.where((mine < counts[0])[:, None], summed * scale, 0.0)


def solution(mesh):
    in_specs = (P("day", None, "pairs", None), P(), P("pairs"), P("pairs", None), P("pairs"))
    out_specs = P(("pairs", "day"), None)
    body = functools.partial(shards, mesh.shape["day"], mesh.shape["pairs"])
    return jax.shard_map(body, mesh=mesh, in_specs=in_specs, out_specs=out_specs, check_vma=False)
```

time: 68.8 us -> 60.7 us (0.88)
  Pallas kernels: 59.4 us -> 51.5 us
    pallas_call x1, Pallas kernels: 59.4 us -> 51.5 us  [shards(): pl.pallas_call(functools.partial(kernel, holders, days, cuts), out_shape=...]
where the time goes in v2:
time: 60.7 us; the launch traced here: 60.5 us
  Pallas kernels  51.5 us (85%)
  local copies, waits for them, and re-layouts  5.31 us (9%)
  other arithmetic  2.98 us (5%)
  between operations  0.72 us (1%)
    pallas_call x1, Pallas kernels, shards(): pl.pallas_call(functools.partial(kernel, holders, days, cuts), out_shape=...  51.5 us
    unnamed x8, local copies, waits for them, and re-layouts  4.87 us

profile of v2, /device:TPU:0, one launch (start us, length us, event | category | flops | bytes accessed | tf_op | source)
XLA Modules:
  0.0 60.5 jit_solution(16544427840464634727)
XLA Ops:
  0.0 0.9 %select_reduce_fusion = s32[16]{0:T(128)S(1)} fusion(s32[256]{0:T(256)} %param.9, s32[16]{0:T(128)} %param.10), kind=kLoop, calls=%fused_computation.6 | loop fusion | flops 12272 | bytes 1152 | tf_op jit(solution)/shard_map/reduce_sum | solution.py:220
  0.9 0.2 convert_reduce_fusion
  1.1 0.1 select_reduce_fusion.1
  1.2 0.1 sub.12
  1.3 0.1 add_select_fusion
  1.3 0.1 select_n.58
  1.5 0.1 broadcast_in_dim.78.req
  1.6 0.1 broadcast_add_fusion.1
  1.6 0.1 add.137
  1.7 0.1 fusion.1.comp
  1.8 0.8 %broadcast_add_fusion = s32[2,2,64]{2,1,0:T(2,128)S(1)} fusion(s32[2,64]{1,0:T(2,128)} %bitcast.5, s32[2]{0:T(128)S(1)} %iota_multiply_fusion), kind=kLoop, calls=%fused_computation.19 | loop fusion | flops 256 | bytes 1544 | tf_op jit(solution)/shard_map/add | solution.py:238
  2.6 0.1 add.141
  2.6 0.1 fusion.sel
  2.7 0.0 copy-start
  2.8 1.7 %copy-done = bf16[1,2,32,18432]{3,2,1,0:T(8,128)(2,1)S(1)} copy-done((bf16[1,2,32,18432]{3,2,1,0:T(8,128)(2,1)S(1)}, bf16[1,2,32,18432]{3,2,1,0:T(8,128)(2,1)}, u32[]{:S(2)}) %copy-start) | copy-done | bytes 2359320
  4.4 0.0 copy-start.1
  4.4 1.4 %copy-done.1 = bf16[768,1024]{1,0:T(8,128)(2,1)S(1)} copy-done((bf16[768,1024]{1,0:T(8,128)(2,1)S(1)}, bf16[768,1024]{1,0:T(8,128)(2,1)}, u32[]{:S(2)}) %copy-start.1) | copy-done | bytes 1572888
  5.8 0.0 copy-start.2
  5.8 0.9 %copy-done.2 = f32[4,2,4608]{2,1,0:T(2,128)S(1)} copy-done((f32[4,2,4608]{2,1,0:T(2,128)S(1)}, f32[4,2,4608]{2,1,0:T(2,128)}, u32[]{:S(2)}) %copy-start.2) | copy-done | bytes 147480
  6.7 0.0 copy-start.3
  6.7 0.9 %copy-done.3 = f32[4,6,2,512]{3,2,1,0:T(2,128)S(1)} copy-done((f32[4,6,2,512]{3,2,1,0:T(2,128)S(1)}, f32[4,6,2,512]{3,2,1,0:T(2,128)}, u32[]{:S(2)}) %copy-start.3) | copy-done | bytes 98328
  7.6 51.5 %shard_map.82 = f32[16,1024]{1,0:T(8,128)S(1)} custom-call(bf16[2,32,18432]{2,1,0:T(8,128)(2,1)S(1)} %bitcast.4, s32[128,128]{1,0:T(8,128)S(1)} %broadcast_in_dim.78.req, bf16[64,128]{1,0:T(8,128)(2,1)S(1)} %fusion.1.comp, bf16[256,32]{1,0:T(8,128)(2,1)S(1)} %fusion.sel, bf16[768,1024]{1,0:T(8,128)(2,1)S(1)} %copy-done.1, f32[4,6,2,512]{3,2,1,0:T(2,128)S(1)} %copy-done.3, ...), custom_call_target="tpu_custom_call" | custom-call | tf_op jit(solution)/shard_map/pallas_call | solution.py:247
  59.8 0.7 %multiply_select_fusion = f32[16,1024]{1,0:T(8,128)} fusion(f32[16,1024]{1,0:T(8,128)S(1)} %shard_map.82, pred[16]{0:T(512)(128)(4,1)S(1)} %add_compare_fusion), kind=kLoop, calls=%fused_computation.2 | loop fusion | flops 32768 | bytes 131088 | tf_op jit(solution)/shard_map/jit(_where)/select_n | solution.py:281
  (8 shorter events, 0.1 us)
Async XLA Ops:
  2.7 1.7 %copy-start = (bf16[1,2,32,18432]{3,2,1,0:T(8,128)(2,1)S(1)}, bf16[1,2,32,18432]{3,2,1,0:T(8,128)(2,1)}, u32[]{:S(2)}) copy-start(bf16[1,2,32,18432]{3,2,1,0:T(8,128)(2,1)} %param.8) | copy-start | bytes 7077892
  4.4 1.4 %copy-start.1 = (bf16[768,1024]{1,0:T(8,128)(2,1)S(1)}, bf16[768,1024]{1,0:T(8,128)(2,1)}, u32[]{:S(2)}) copy-start(bf16[768,1024]{1,0:T(8,128)(2,1)} %constant.56.clone.table_hbm) | copy-start | bytes 4718596
  5.8 0.9 %copy-start.2 = (f32[4,2,4608]{2,1,0:T(2,128)S(1)}, f32[4,2,4608]{2,1,0:T(2,128)}, u32[]{:S(2)}) copy-start(f32[4,2,4608]{2,1,0:T(2,128)} %constant.58.clone.turn_hbm) | copy-start | bytes 442372
  6.7 0.9 %copy-start.3 = (f32[4,6,2,512]{3,2,1,0:T(2,128)S(1)}, f32[4,6,2,512]{3,2,1,0:T(2,128)}, u32[]{:S(2)}) copy-start(f32[4,6,2,512]{3,2,1,0:T(2,128)} %constant.57.clone.outer_hbm) | copy-start | bytes 294916

commit v3 on v2

--- a/solution.py
+++ b/solution.py
@@ -272,7 +272,7 @@
             dma((days,)), dma((days,)),
         ],
         compiler_params=pltpu.CompilerParams(
-            collective_id=0, has_side_effects=True, vmem_limit_bytes=48 * 2**20
+            collective_id=0, has_side_effects=True, vmem_limit_bytes=63 * 2**20
         ),
     )(spectra[0], req, comp, sel, jnp.asarray(table), jnp.asarray(outer), jnp.asarray(turn))
     share = slots // days

time: 60.7 us -> 59.4 us (0.979)
  local copies, waits for them, and re-layouts: 5.31 us -> 1.08 us
  other arithmetic: 2.98 us -> 5.03 us
  Pallas kernels: 51.5 us -> 52.3 us
    unnamed x8 -> x0, local copies, waits for them, and re-layouts: 4.87 us -> none
    pallas_call x1, Pallas kernels: 51.5 us -> 52.3 us  [shards(): pl.pallas_call(functools.partial(kernel, holders, days, cuts), out_shape=...]
    select_n x1, other arithmetic: 0.7 us -> 1.54 us  [shards(): return jnp.where((mine < counts[0])[:, None], summed * scale, 0.0)]
    broadcast_in_dim x1, local copies, waits for them, and re-layouts: 0.07 us -> 0.72 us  [shards(): jnp.broadcast_to(req.reshape(holders * 16, 1), (holders * 16, 4 * stations))]
    convert_element_type x1, other arithmetic: 0.1 us -> 0.72 us  [shards(): sel = sel.astype(jnp.bfloat16)]
where the time goes in v3:
time: 59.4 us; the launch traced here: 59.1 us
  Pallas kernels  52.3 us (88%)
  other arithmetic  5.03 us (8%)
  local copies, waits for them, and re-layouts  1.08 us (2%)
  between operations  0.69 us (1%)
    pallas_call x1, Pallas kernels, shards(): pl.pallas_call(functools.partial(kernel, holders, days, cuts), out_shape=...  52.3 us
    select_n x1, other arithmetic, shards(): return jnp.where((mine < counts[0])[:, None], summed * scale, 0.0)  1.54 us

profile of v3, /device:TPU:0, one launch (start us, length us, event | category | flops | bytes accessed | tf_op | source)
XLA Modules:
  0.0 59.1 jit_solution(10451411970031033378)
XLA Ops:
  0.0 0.9 %select_reduce_fusion = s32[16]{0:T(128)S(1)} fusion(s32[256]{0:T(256)} %param.9, s32[16]{0:T(128)} %param.10), kind=kLoop, calls=%fused_computation.6 | loop fusion | flops 12272 | bytes 1152 | tf_op jit(solution)/shard_map/reduce_sum | solution.py:220
  0.9 0.2 convert_reduce_fusion
  1.1 0.1 select_reduce_fusion.1
  1.2 0.1 sub.12
  1.3 0.1 add_select_fusion
  1.3 0.1 select_n.58
  1.5 0.7 %broadcast_in_dim.78.req = s32[128,128]{1,0:T(8,128)} broadcast(s32[128]{0:T(128)S(1)} %select_n.58), dimensions={0} | broadcast | bytes 66048 | tf_op jit(solution)/shard_map/broadcast_in_dim | solution.py:233
  2.2 0.1 broadcast_add_fusion.1
  2.3 0.1 add.137
  2.3 0.7 %fusion.1.comp = bf16[64,128]{1,0:T(8,128)(2,1)} fusion(s32[64]{0:T(128)S(1)} %add.137), kind=kLoop, calls=%fused_computation.4 | loop fusion | flops 16384 | bytes 16640 | tf_op jit(solution)/shard_map/convert_element_type | solution.py:237
  3.0 0.7 %broadcast_add_fusion = s32[2,2,64]{2,1,0:T(2,128)S(1)} fusion(s32[2,64]{1,0:T(2,128)} %bitcast.5, s32[2]{0:T(128)S(1)} %iota_multiply_fusion), kind=kLoop, calls=%fused_computation.19 | loop fusion | flops 256 | bytes 1544 | tf_op jit(solution)/shard_map/add | solution.py:238
  3.8 0.1 add.141
  3.9 0.7 %fusion.sel = bf16[256,32]{1,0:T(8,128)(2,1)} fusion(s32[256]{0:T(256)S(1)} %add.141), kind=kLoop, calls=%fused_computation.1 | loop fusion | flops 16384 | bytes 17408 | tf_op jit(solution)/shard_map/convert_element_type | solution.py:240
  4.6 52.3 %shard_map.82 = f32[16,1024]{1,0:T(8,128)} custom-call(bf16[2,32,18432]{2,1,0:T(8,128)(2,1)} %bitcast.4, s32[128,128]{1,0:T(8,128)} %broadcast_in_dim.78.req, bf16[64,128]{1,0:T(8,128)(2,1)} %fusion.1.comp, bf16[256,32]{1,0:T(8,128)(2,1)} %fusion.sel, bf16[768,1024]{1,0:T(8,128)(2,1)} %constant.56.clone.table_hbm, ...), custom_call_target="tpu_custom_call" | custom-call | tf_op jit(solution)/shard_map/pallas_call | solution.py:247
  57.6 1.5 %multiply_select_fusion = f32[16,1024]{1,0:T(8,128)} fusion(f32[16,1024]{1,0:T(8,128)} %shard_map.82, pred[16]{0:T(512)(128)(4,1)S(1)} %add_compare_fusion), kind=kLoop, calls=%fused_computation.2 | loop fusion | flops 32768 | bytes 131088 | tf_op jit(solution)/shard_map/jit(_where)/select_n | solution.py:281
  (8 shorter events, 0.1 us)
